TPU v7x, 32 devices: a whole 2x2x4 slice. The times are simulated.
32 devices in a mesh: tm: 4 (over y, x), band: 8 (over z, core).
Axes of the slice: x: 2, y: 2, z: 4, core: 2. Of those that a mesh axis runs over, the one named last changes fastest.
Arguments:
- increments: float32 [4, 4, 2, 1024, 1024], P('tm', None, None, 'band'), may hold values from -6 to 6
- velocity: float32 [4, 2, 1024, 1024], P('tm', None, 'band'), may hold values from -0.4 to 0.4
- diffusivity: float32 [4, 2], replicated, may hold values from 0.03 to 0.22
- scaling: float32 [4, 2, 1024, 1024], P(None, None, 'band'), may hold values from 0.3 to 3
- correlation: float32 [1024, 1024], P('band'), may hold values from -0.2 to 0.5
Outputs:
- weighted_defects: float32 [4, 4, 2, 1024, 1024], P('tm', None, None, 'band')
All inputs are finite; a program needn't handle non-finite values.
Results may differ from a plain program's by a relative error of at most 0.000094.
Values sent between devices are 32-bit elements; how exact they have to be, the bound alone decides.
A program may use at most 64 MiB of HBM per device.

v0:
```python
import functools
import math

import jax
import jax.numpy as jnp
from jax import lax
from jax.experimental import pallas as pl
from jax.experimental.pallas import tpu as pltpu
from jax.sharding import PartitionSpec as P

FIELDS = 4
LEVELS = 2
STEPS = 4
HALO = 8
LANES = 128
LAG = 2
MESH = pl.DeviceIdType.MESH
VMEM_LIMIT = 52 * 1024 * 1024


def greet(band_size, tm_size, with_tm):
    me = lax.axis_index("band")
    window = lax.axis_index("tm")
    barrier = pltpu.get_barrier_semaphore()
    for d in range(1, band_size):
        pl.semaphore_signal(
            barrier, inc=1, device_id={"band": lax.rem(me + d, band_size)}, device_id_type=MESH
        )
    if with_tm:

        @pl.when(window > 0)
        def _():
            pl.semaphore_signal(barrier, inc=1, device_id={"tm": window - 1}, device_id_type=MESH)

        @pl.when(window < tm_size - 1)
        def _():
            pl.semaphore_signal(barrier, inc=1, device_id={"tm": window + 1}, device_id_type=MESH)

    peers = band_size - 1
    if with_tm:
        peers = peers + (window > 0).astype(jnp.int32) + (window < tm_size - 1).astype(jnp.int32)
    pl.semaphore_wait(barrier, peers)


def spread_kernel(
    band_size, tm_size, group,
    inc, vel, diff, sig,
    recv,
    ends, arrived, scaled, ping, pong, east_speed, north_speed, halo_x, halo_v,
    halo_send, halo_recv, tm_send, tm_recv, a2a_send, a2a_recv, own_sem,
):
    channels, rows, width = inc.shape
    pieces = band_size // group
    piece_width = width // pieces
    steps = channels // group
    me = lax.axis_index("band")
    window = lax.axis_index("tm")

    greet(band_size, tm_size, True)

    def halo_copies(side, neighbour):
        own = pl.ds(0, HALO) if side else pl.ds(rows - HALO, HALO)
        return [
            pltpu.make_async_remote_copy(
                src_ref=array.at[:, own, :],
                dst_ref=store.at[side],
                send_sem=halo_send.at[side, kind],
                recv_sem=halo_recv.at[side, kind],
                device_id={"band": neighbour},
                device_id_type=MESH,
            )
            for kind, (array, store) in enumerate(((vel, halo_v), (inc, halo_x)))
        ]

    @pl.when(me > 0)
    def _():
        for copy in halo_copies(1, me - 1):
            copy.start()

    @pl.when(me < band_size - 1)
    def _():
        for copy in halo_copies(0, me + 1):
            copy.start()

    zeros = jnp.zeros((HALO, width), jnp.float32)
    for store in (ping, pong):
        store[pl.ds(0, HALO), :] = zeros
        store[pl.ds(rows + 3 * HALO, HALO), :] = zeros

    @pl.when(me == 0)
    def _():
        halo_x[0] = jnp.zeros(halo_x.shape[1:], jnp.float32)
        halo_v[0] = jnp.zeros(halo_v.shape[1:], jnp.float32)

    @pl.when(me == band_size - 1)
    def _():
        halo_x[1] = jnp.zeros(halo_x.shape[1:], jnp.float32)
        halo_v[1] = jnp.zeros(halo_v.shape[1:], jnp.float32)

    def inner_speeds(j, carry):
        at = pl.multiple_of(j * HALO, HALO)
        east_speed[pl.ds(at + 2 * HALO, HALO), :] = 0.5 * vel[0, pl.ds(at, HALO), :]
        north_speed[pl.ds(at + 2 * HALO, HALO), :] = 0.5 * vel[1, pl.ds(at, HALO), :]
        return carry

    lax.fori_loop(0, rows // HALO, inner_speeds, 0)

    @pl.when(me > 0)
    def _():
        for copy in halo_copies(0, me - 1):
            copy.wait_recv()

    @pl.when(me < band_size - 1)
    def _():
        for copy in halo_copies(1, me + 1):
            copy.wait_recv()

    for side, at in ((0, HALO), (1, rows + 2 * HALO)):
        east_speed[pl.ds(at, HALO), :] = 0.5 * halo_v[side, 0]
        north_speed[pl.ds(at, HALO), :] = 0.5 * halo_v[side, 1]

    def tangent_step(src, k, first, count, put):
        def strip(j, carry):
            at = pl.multiple_of((first + j) * HALO, HALO)
            near = src[pl.ds(pl.multiple_of(at - HALO, HALO), 3 * HALO), :]
            now = near[HALO : 2 * HALO]
            upper = pltpu.roll(near, 3 * HALO - 1, 0)[HALO : 2 * HALO]
            lower = pltpu.roll(near, 1, 0)[HALO : 2 * HALO]
            eastern = pltpu.roll(now, width - 1, 1)
            western = pltpu.roll(now, 1, 1)
            after = (
                now
                - east_speed[pl.ds(at, HALO), :] * (eastern - western)
                - north_speed[pl.ds(at, HALO), :] * (upper - lower)
                + k * (upper + lower + eastern + western - 4.0 * now)
            )
            place = me * (rows // HALO) + first + j - 2
            inside = (place >= 0) & (place < band_size * (rows // HALO))
            put(at, after * jnp.where(inside, 1.0, 0.0))
            return carry

        lax.fori_loop(0, count, strip, 0)

    def propagate(f):
        k = diff[f]

        def fill(j, carry):
            at = pl.multiple_of(j * HALO, HALO)
            ping[pl.ds(at + 2 * HALO, HALO), :] = inc[f, pl.ds(at, HALO), :]
            return carry

        lax.fori_loop(0, rows // HALO, fill, 0)
        ping[pl.ds(HALO, HALO), :] = halo_x[0, f]
        ping[pl.ds(rows + 2 * HALO, HALO), :] = halo_x[1, f]
        stores = (ping, pong)
        for section in range(STEPS - 1):
            target = stores[(section + 1) % 2]

            def put(at, value, target=target):
                target[pl.ds(at, HALO), :] = value

            tangent_step(stores[section % 2], k, 1, rows // HALO + 2, put)

        def put_end(at, value):
            ends[f, pl.ds(pl.multiple_of(at - 2 * HALO, HALO), HALO), :] = value

        tangent_step(stores[(STEPS - 1) % 2], k, 2, rows // HALO, put_end)

    def tm_copy(f, other):
        return pltpu.make_async_remote_copy(
            src_ref=ends.at[f],
            dst_ref=arrived.at[f],
            send_sem=tm_send.at[f],
            recv_sem=tm_recv.at[f],
            device_id={"tm": other},
            device_id_type=MESH,
        )

    def block_copy(step, block, owner, other):
        return pltpu.make_async_remote_copy(
            src_ref=scaled.at[step, block],
            dst_ref=recv.at[step, pl.ds(pl.multiple_of(owner * rows, rows), rows), :],
            send_sem=a2a_send.at[step, block],
            recv_sem=a2a_recv.at[step, owner],
            device_id={"band": other},
            device_id_type=MESH,
        )

    def own_copy(step):
        return pltpu.make_async_copy(
            scaled.at[step, me],
            recv.at[step, pl.ds(pl.multiple_of(me * rows, rows), rows), :],
            own_sem.at[step],
        )

    def turn(i, carry):
        @pl.when((i < channels) & (window < tm_size - 1))
        def _():
            propagate(i)
            tm_copy(i, window + 1).start()

        @pl.when(i >= LAG)
        def _():
            f = i - LAG
            step, part = f // group, lax.rem(f, group)

            @pl.when(window > 0)
            def _():
                tm_copy(f, window - 1).wait_recv()
                for p in range(pieces):
                    cut = pl.ds(p * piece_width, piece_width)
                    scaled[step, part * pieces + p] = sig[f, :, cut] * (inc[f, :, cut] - arrived[f, :, cut])

            @pl.when(window == 0)
            def _():
                for p in range(pieces):
                    cut = pl.ds(p * piece_width, piece_width)
                    scaled[step, part * pieces + p] = sig[f, :, cut] * inc[f, :, cut]

            for p in range(pieces):
                block = part * pieces + lax.rem(me + p, pieces)

                @pl.when(block != me)
                def _(block=block):
                    block_copy(step, block, me, block).start()

                @pl.when(block == me)
                def _():
                    own_copy(step).start()

        return carry

    lax.fori_loop(0, channels + LAG, turn, 0)

    def finish(step, carry):
        for d in range(1, band_size):
            other = lax.rem(me + d, band_size)
            block_copy(step, other, me, other).wait_send()
            block_copy(step, other, other, other).wait_recv()
        own_copy(step).wait()
        return carry

    lax.fori_loop(0, steps, finish, 0)

    @pl.when(window < tm_size - 1)
    def _():
        def sent(f, carry):
            tm_copy(f, window + 1).wait_send()
            return carry

        lax.fori_loop(0, channels, sent, 0)

    @pl.when(me > 0)
    def _():
        for copy in halo_copies(1, me - 1):
            copy.wait_send()

    @pl.when(me < band_size - 1)
    def _():
        for copy in halo_copies(0, me + 1):
            copy.wait_send()


def halves(value):
    high = value.astype(jnp.bfloat16)
    return high, (value - high.astype(jnp.float32)).astype(jnp.bfloat16)


def correlate_kernel(
    band_size, group,
    blocks, corr, sig,
    out,
    high, low, mixed, back, send_sem, recv_sem,
):
    steps, order, piece_width = blocks.shape
    channels, rows, width = sig.shape
    pieces = band_size // group
    me = lax.axis_index("band")
    tile = min(order, 512)

    greet(band_size, 1, False)

    def split(j, carry):
        at = pl.multiple_of(j * 64, 64)
        high[pl.ds(at, 64), :], low[pl.ds(at, 64), :] = halves(corr[pl.ds(at, 64), :])
        return carry

    lax.fori_loop(0, order // 64, split, 0)

    def block_copy(step, owner, other):
        return pltpu.make_async_remote_copy(
            src_ref=mixed.at[step, pl.ds(pl.multiple_of(other * rows, rows), rows), :],
            dst_ref=back.at[step, owner],
            send_sem=send_sem.at[step, other],
            recv_sem=recv_sem.at[step, owner],
            device_id={"band": other},
            device_id_type=MESH,
        )

    def along_rows(step, carry):
        s_high, s_low = halves(blocks[step])
        both = jnp.concatenate([s_high, s_low], axis=1)

        def row_tile(j, carry):
            at = pl.multiple_of(j * tile, tile)
            one = jnp.dot(high[pl.ds(at, tile), :], both, preferred_element_type=jnp.float32)
            two = jnp.dot(low[pl.ds(at, tile), :], s_high, preferred_element_type=jnp.float32)
            mixed[step, pl.ds(at, tile), :] = one[:, :piece_width] + (one[:, piece_width:] + two)
            return carry

        lax.fori_loop(0, order // tile, row_tile, 0)
        for d in range(1, band_size):
            block_copy(step, me, lax.rem(me + d, band_size)).start()
        back[step, me] = mixed[step, pl.ds(pl.multiple_of(me * rows, rows), rows), :]
        return carry

    lax.fori_loop(0, steps, along_rows, 0)

    contract_last = (((1,), (1,)), ((), ()))

    def along_columns(f, carry):
        step, part = f // group, lax.rem(f, group)
        for p in range(pieces):
            owner = part * pieces + p

            @pl.when(owner != me)
            def _(owner=owner):
                block_copy(step, owner, owner).wait_recv()

        value = jnp.concatenate([back[step, part * pieces + p] for p in range(pieces)], axis=1)
        v_high, v_low = halves(value)
        both = jnp.concatenate([v_high, v_low], axis=0)
        for j in range(width // tile):
            cut = pl.ds(j * tile, tile)
            one = lax.dot_general(both, high[cut, :], contract_last, preferred_element_type=jnp.float32)
            two = lax.dot_general(v_high, low[cut, :], contract_last, preferred_element_type=jnp.float32)
            out[f, :, cut] = sig[f, :, cut] * (one[:rows] + (one[rows:] + two))
        return carry

    lax.fori_loop(0, channels, along_columns, 0)

    def sent(step, carry):
        for d in range(1, band_size):
            block_copy(step, me, lax.rem(me + d, band_size)).wait_send()
        return carry

    lax.fori_loop(0, steps, sent, 0)


def local(increments, velocity, diffusivity, scaling, correlation):
    band_size, tm_size = lax.axis_size("band"), lax.axis_size("tm")
    rows, width = increments.shape[3:]
    channels = FIELDS * LEVELS
    inc = increments.reshape(channels, rows, width)
    sig = scaling.reshape(channels, rows, width)
    diff = diffusivity.reshape(channels)
    group = max(1, LANES * band_size // width)
    steps = channels // group
    piece_width = width * group // band_size
    order = rows * band_size
    dma = pltpu.SemaphoreType.DMA
    f32 = jnp.float32
    vmem = pl.BlockSpec(memory_space=pltpu.VMEM)

    share = math.gcd(rows, tm_size)
    if share == tm_size:
        part = rows // tm_size
        mine = lax.dynamic_slice_in_dim(correlation, lax.axis_index("tm") * part, part, 0)
        corr = lax.all_gather(mine, ("band", "tm"), axis=0, tiled=True)
    else:
        corr = lax.all_gather(correlation, "band", axis=0, tiled=True)

    blocks = pl.pallas_call(
        functools.partial(spread_kernel, band_size, tm_size, group),
        out_shape=jax.ShapeDtypeStruct((steps, order, piece_width), f32),
        in_specs=[vmem, vmem, pl.BlockSpec(memory_space=pltpu.SMEM), vmem],
        out_specs=pl.BlockSpec(memory_space=pl.ANY),
        scratch_shapes=[
            pltpu.VMEM((channels, rows, width), f32),
            pltpu.VMEM((channels, rows, width), f32),
            pltpu.VMEM((steps, band_size, rows, piece_width), f32),
            pltpu.VMEM((rows + 4 * HALO, width), f32),
            pltpu.VMEM((rows + 4 * HALO, width), f32),
            pltpu.VMEM((rows + 4 * HALO, width), f32),
            pltpu.VMEM((rows + 4 * HALO, width), f32),
            pltpu.VMEM((2, channels, HALO, width), f32),
            pltpu.VMEM((2, 2, HALO, width), f32),
            dma((2, 2)),
            dma((2, 2)),
            dma((channels,)),
            dma((channels,)),
            dma((steps, band_size)),
            dma((steps, band_size)),
            dma((steps,)),
        ],
        compiler_params=pltpu.CompilerParams(
            collective_id=0, has_side_effects=True, vmem_limit_bytes=VMEM_LIMIT
        ),
        cost_estimate=pl.CostEstimate(
            flops=200 * channels * rows * width, bytes_accessed=128 * channels * rows * width, transcendentals=0
        ),
        name="spread",
    )(inc, velocity[0], diff, sig)

    out = pl.pallas_call(
        functools.partial(correlate_kernel, band_size, group),
        out_shape=jax.ShapeDtypeStruct((channels, rows, width), f32),
        in_specs=[vmem, vmem, vmem],
        out_specs=vmem,
        scratch_shapes=[
            pltpu.VMEM((order, order), jnp.bfloat16),
            pltpu.VMEM((order, order), jnp.bfloat16),
            pltpu.VMEM((steps, order, piece_width), f32),
            pltpu.VMEM((steps, band_size, rows, piece_width), f32),
            dma((steps, band_size)),
            dma((steps, band_size)),
        ],
        compiler_params=pltpu.CompilerParams(
            collective_id=1, has_side_effects=True, vmem_limit_bytes=VMEM_LIMIT
        ),
        cost_estimate=pl.CostEstimate(
            flops=12 * channels * rows * width * order, bytes_accessed=16 * channels * rows * width, transcendentals=0
        ),
        name="correlate",
    )(blocks, corr, sig)
    return out.reshape(1, FIELDS, LEVELS, rows, width)


def solution(mesh):
    return jax.shard_map(
        local,
        mesh=mesh,
        in_specs=(
            P("tm", None, None, "band", None),
            P("tm", None, "band", None),
            P(),
            P(None, None, "band", None),
            P("band", None),
        ),
        out_specs=P("tm", None, None, "band", None),
        check_vma=False,
    )
```

profile of v0, /device:TPU:29, one launch (start us, length us, event | category | flops | bytes accessed | tf_op | source)
XLA Modules:
  0.0 265.4 jit_solution(10195978905743658112)
XLA Ops:
  6.5 0.0 copy-start
  6.5 0.0 all-gather.2.cloned.1.call-start
  6.5 1.0 copy-done
  7.6 0.7 constant_dynamic-slice_fusion
  8.2 0.0 all-gather.2.cloned.1.call-update
  8.3 0.8 copy.7
  9.0 0.1 reshape.13.diff
  9.1 0.0 copy-start.1
  9.1 1.2 copy-done.1
  10.3 138.5 %spread.1.blocks = f32[8,1024,128]{2,1,0:T(8,128)} custom-call(f32[8,128,1024]{2,1,0:T(8,128)} %bitcast.6, f32[2,128,1024]{2,1,0:T(8,128)S(1)} %bitcast.4, f32[8]{0:T(128)S(1)} %reshape.13.diff, f32[8,128,1024]{2,1,0:T(8,128)} %bitcast.7), custom_call_target="tpu_custom_call" | custom-call | flops 209715200 | bytes 134217728 | tf_op jit(solution)/shard_map/spread/pallas_call | solution.py:373
  148.8 0.0 all-gather.2.cloned.1.call-done.corr
  148.8 104.9 %correlate.1 = f32[8,128,1024]{2,1,0:T(8,128)} custom-call(f32[8,1024,128]{2,1,0:T(8,128)} %spread.1.blocks, f32[1024,1024]{1,0:T(8,128)} %all-gather.2.cloned.1.call-done.corr, f32[8,128,1024]{2,1,0:T(8,128)} %bitcast.8), custom_call_target="tpu_custom_call" | custom-call | flops 12884901888 | bytes 16777216 | tf_op jit(solution)/shard_map/correlate/pallas_call | solution.py:405
  253.7 4.8 %copy.9 = f32[1,4,2,128,1024]{4,3,2,1,0:T(8,128)} copy(f32[1,4,2,128,1024]{4,3,2,1,0:T(8,128)} %bitcast.5) | data formatting | bytes 8388608
Async XLA Ops:
  6.5 1.0 copy-start
  6.5 142.3 %all-gather.2.cloned.1.call-start = ((), (), s32[]{:S(2)}) async-start(), calls=%async_computation | async-start | bytes 4325376 | tf_op jit(solution)/shard_map/all_gather | solution.py:369
  9.1 1.2 copy-start.1
Sparse Core Ops, SparseCore 0:
  10.2 78.0 all-gather.1
where the time goes:
time: 266 us; the launch traced here: 265 us
  Pallas kernels  243 us (91%)
  between operations  13.4 us (5%)
  local copies, waits for them, and re-layouts  8.57 us (3%)
    pallas_call x1, Pallas kernels, local(): pl.pallas_call(functools.partial(spread_kernel, band_size, tm_size, group...  138 us
    pallas_call x1, Pallas kernels, local(): pl.pallas_call(functools.partial(correlate_kernel, band_size, group), out...  105 us
    unnamed x6, local copies, waits for them, and re-layouts  7.82 us
  transfers between devices with their start and end apart: 1, of which 0 were waited for; matrix products, arithmetic and copies ran while one was open for 0% of the time, Pallas kernels for 52%

commit v1 on v0

--- a/solution.py
+++ b/solution.py
@@ -139,7 +139,8 @@
             put(at, after * jnp.where(inside, 1.0, 0.0))
             return carry
 
-        lax.fori_loop(0, count, strip, 0)
+        unroll = max(n for n in range(1, 7) if count % n == 0)
+        lax.fori_loop(0, count, strip, 0, unroll=unroll)
 
     def propagate(f):
         k = diff[f]
@@ -149,7 +150,7 @@
             ping[pl.ds(at + 2 * HALO, HALO), :] = inc[f, pl.ds(at, HALO), :]
             return carry
 
-        lax.fori_loop(0, rows // HALO, fill, 0)
+        lax.fori_loop(0, rows // HALO, fill, 0, unroll=4)
         ping[pl.ds(HALO, HALO), :] = halo_x[0, f]
         ping[pl.ds(rows + 2 * HALO, HALO), :] = halo_x[1, f]
         stores = (ping, pong)

time: 266 us -> 261 us (0.981)
  Pallas kernels: 243 us -> 238 us
    pallas_call x1, Pallas kernels: 138 us -> 133 us  [local(): pl.pallas_call(functools.partial(spread_kernel, band_size, tm_size, group...]
  transfers between devices with their start and end apart: 1 -> 1, of which waited for: 0 -> 0; matrix products, arithmetic and copies ran while one was open for 0% -> 0% of each run, Pallas kernels for 52% -> 51%
where the time goes in v1:
time: 261 us; the launch traced here: 260 us
  Pallas kernels  238 us (91%)
  between operations  13.4 us (5%)
  local copies, waits for them, and re-layouts  8.57 us (3%)
    pallas_call x1, Pallas kernels, local(): pl.pallas_call(functools.partial(spread_kernel, band_size, tm_size, group...  133 us
    pallas_call x1, Pallas kernels, local(): pl.pallas_call(functools.partial(correlate_kernel, band_size, group), out...  105 us
    unnamed x6, local copies, waits for them, and re-layouts  7.82 us
  transfers between devices with their start and end apart: 1, of which 0 were waited for; matrix products, arithmetic and copies ran while one was open for 0% of the time, Pallas kernels for 51%

profile of v1, /device:TPU:29, one launch (start us, length us, event | category | flops | bytes accessed | tf_op | source)
XLA Modules:
  0.0 260.2 jit_solution(5595696478253518188)
XLA Ops:
  6.5 0.0 copy-start
  6.5 0.0 all-gather.2.cloned.1.call-start
  6.5 1.0 copy-done
  7.6 0.7 constant_dynamic-slice_fusion
  8.2 0.0 all-gather.2.cloned.1.call-update
  8.3 0.8 copy.7
  9.0 0.1 reshape.13.diff
  9.1 0.0 copy-start.1
  9.1 1.2 copy-done.1
  10.3 133.3 %spread.1.blocks = f32[8,1024,128]{2,1,0:T(8,128)} custom-call(f32[8,128,1024]{2,1,0:T(8,128)} %bitcast.6, f32[2,128,1024]{2,1,0:T(8,128)S(1)} %bitcast.4, f32[8]{0:T(128)S(1)} %reshape.13.diff, f32[8,128,1024]{2,1,0:T(8,128)} %bitcast.7), custom_call_target="tpu_custom_call" | custom-call | flops 209715200 | bytes 134217728 | tf_op jit(solution)/shard_map/spread/pallas_call | solution.py:374
  143.6 0.0 all-gather.2.cloned.1.call-done.corr
  143.7 104.9 %correlate.1 = f32[8,128,1024]{2,1,0:T(8,128)} custom-call(f32[8,1024,128]{2,1,0:T(8,128)} %spread.1.blocks, f32[1024,1024]{1,0:T(8,128)} %all-gather.2.cloned.1.call-done.corr, f32[8,128,1024]{2,1,0:T(8,128)} %bitcast.8), custom_call_target="tpu_custom_call" | custom-call | flops 12884901888 | bytes 16777216 | tf_op jit(solution)/shard_map/correlate/pallas_call | solution.py:406
  248.6 4.8 %copy.9 = f32[1,4,2,128,1024]{4,3,2,1,0:T(8,128)} copy(f32[1,4,2,128,1024]{4,3,2,1,0:T(8,128)} %bitcast.5) | data formatting | bytes 8388608
Async XLA Ops:
  6.5 1.0 copy-start
  6.5 137.1 %all-gather.2.cloned.1.call-start = ((), (), s32[]{:S(2)}) async-start(), calls=%async_computation | async-start | bytes 4325376 | tf_op jit(solution)/shard_map/all_gather | solution.py:370
  9.1 1.2 copy-start.1
Sparse Core Ops, SparseCore 0:
  10.2 78.6 all-gather.1

commit v2 on v1

--- a/solution.py
+++ b/solution.py
@@ -1,5 +1,4 @@
 import functools
-import math
 
 import jax
 import jax.numpy as jnp
@@ -14,40 +13,50 @@
 HALO = 8
 LANES = 128
 LAG = 2
+BACK_LAG = 4
 MESH = pl.DeviceIdType.MESH
-VMEM_LIMIT = 52 * 1024 * 1024
-
-
-def greet(band_size, tm_size, with_tm):
+VMEM_LIMIT = 60 * 1024 * 1024
+
+
+def greet(band_size, tm_size, sharers):
     me = lax.axis_index("band")
     window = lax.axis_index("tm")
+    base = window - lax.rem(window, sharers)
     barrier = pltpu.get_barrier_semaphore()
     for d in range(1, band_size):
         pl.semaphore_signal(
             barrier, inc=1, device_id={"band": lax.rem(me + d, band_size)}, device_id_type=MESH
         )
-    if with_tm:
-
-        @pl.when(window > 0)
-        def _():
-            pl.semaphore_signal(barrier, inc=1, device_id={"tm": window - 1}, device_id_type=MESH)
-
-        @pl.when(window < tm_size - 1)
-        def _():
-            pl.semaphore_signal(barrier, inc=1, device_id={"tm": window + 1}, device_id_type=MESH)
-
-    peers = band_size - 1
-    if with_tm:
-        peers = peers + (window > 0).astype(jnp.int32) + (window < tm_size - 1).astype(jnp.int32)
+    for d in range(1, sharers):
+        other = base + lax.rem(window - base + d, sharers)
+        pl.semaphore_signal(barrier, inc=1, device_id={"tm": other}, device_id_type=MESH)
+    before = (window > 0) & (window == base)
+    after = (window < tm_size - 1) & (window == base + sharers - 1)
+
+    @pl.when(before)
+    def _():
+        pl.semaphore_signal(barrier, inc=1, device_id={"tm": window - 1}, device_id_type=MESH)
+
+    @pl.when(after)
+    def _():
+        pl.semaphore_signal(barrier, inc=1, device_id={"tm": window + 1}, device_id_type=MESH)
+
+    peers = band_size - 1 + sharers - 1 + before.astype(jnp.int32) + after.astype(jnp.int32)
     pl.semaphore_wait(barrier, peers)
 
 
-def spread_kernel(
-    band_size, tm_size, group,
-    inc, vel, diff, sig,
-    recv,
-    ends, arrived, scaled, ping, pong, east_speed, north_speed, halo_x, halo_v,
-    halo_send, halo_recv, tm_send, tm_recv, a2a_send, a2a_recv, own_sem,
+def halves(value):
+    high = value.astype(jnp.bfloat16)
+    return high, (value - high.astype(jnp.float32)).astype(jnp.bfloat16)
+
+
+def defects_kernel(
+    band_size, tm_size, group, sharers,
+    inc, vel, diff, sig, corr,
+    out,
+    full, high, low, mixed, back, recv, ends, arrived, scaled, ping, pong, east_speed, north_speed, halo_x, halo_v,
+    halo_send, halo_recv, tm_send, tm_recv, a2a_send, a2a_recv, own_sem, back_send, back_recv,
+    share_send, share_recv, window_send, window_recv, core_send, core_recv,
 ):
     channels, rows, width = inc.shape
     pieces = band_size // group
@@ -56,7 +65,16 @@
     me = lax.axis_index("band")
     window = lax.axis_index("tm")
 
-    greet(band_size, tm_size, True)
+    order = band_size * rows
+    part = rows // sharers
+    tile = min(order, 512)
+    pairs = band_size // 2
+    chip, core = me // 2, lax.rem(me, 2)
+    sibling = me + 1 - 2 * core
+    turn_in = lax.rem(window, sharers)
+    base = window - turn_in
+
+    greet(band_size, tm_size, sharers)
 
     def halo_copies(side, neighbour):
         own = pl.ds(0, HALO) if side else pl.ds(rows - HALO, HALO)
@@ -81,6 +99,79 @@
     def _():
         for copy in halo_copies(0, me + 1):
             copy.start()
+
+    def source(h):
+        return 2 * lax.rem(chip - h + pairs, pairs) + core
+
+    def share_rows(band, share):
+        return pl.ds(pl.multiple_of(band * rows + share * part, part), part)
+
+    def band_rows(band):
+        return pl.ds(pl.multiple_of(band * rows, rows), rows)
+
+    def share_copy(h, owner, other):
+        return pltpu.make_async_remote_copy(
+            src_ref=corr.at[pl.ds(pl.multiple_of(turn_in * part, part), part), :],
+            dst_ref=full.at[share_rows(owner, turn_in), :],
+            send_sem=share_send.at[h],
+            recv_sem=share_recv.at[h],
+            device_id={"band": other},
+            device_id_type=MESH,
+        )
+
+    def window_copy(h, g, share, other):
+        at = share_rows(source(h), share)
+        return pltpu.make_async_remote_copy(
+            src_ref=full.at[at, :],
+            dst_ref=full.at[at, :],
+            send_sem=window_send.at[h, g],
+            recv_sem=window_recv.at[h, g],
+            device_id={"tm": other},
+            device_id_type=MESH,
+        )
+
+    def core_copy(h, owner):
+        at = band_rows(owner)
+        return pltpu.make_async_remote_copy(
+            src_ref=corr if h == 0 else full.at[at, :],
+            dst_ref=full.at[at, :],
+            send_sem=core_send.at[h],
+            recv_sem=core_recv.at[h],
+            device_id={"band": sibling},
+            device_id_type=MESH,
+        )
+
+    def onward(h):
+        return 2 * lax.rem(chip + h, pairs) + core
+
+    for h in range(1, pairs):
+        share_copy(h, me, onward(h)).start()
+    core_copy(0, me).start()
+
+    def pass_to_windows():
+        for h in range(1, pairs):
+            share_copy(h, source(h), source(h)).wait_recv()
+            for g in range(1, sharers):
+                window_copy(h, g, turn_in, base + lax.rem(turn_in + g, sharers)).start()
+
+    def pass_to_sibling():
+        for h in range(1, pairs):
+            for g in range(1, sharers):
+                share = lax.rem(turn_in - g + sharers, sharers)
+                window_copy(h, g, share, base + share).wait_recv()
+            core_copy(h, source(h)).start()
+
+    def split_matrix():
+        full[band_rows(me), :] = corr[...]
+        for h in range(pairs):
+            core_copy(h, source(h) + 1 - 2 * core).wait_recv()
+
+        def split(j, carry):
+            at = pl.multiple_of(j * 64, 64)
+            high[pl.ds(at, 64), :], low[pl.ds(at, 64), :] = halves(full[pl.ds(at, 64), :])
+            return carry
+
+        lax.fori_loop(0, order // 64, split, 0)
 
     zeros = jnp.zeros((HALO, width), jnp.float32)
     for store in (ping, pong):
@@ -194,13 +285,43 @@
             own_sem.at[step],
         )
 
+    def back_copy(step, owner, other):
+        return pltpu.make_async_remote_copy(
+            src_ref=mixed.at[step, pl.ds(pl.multiple_of(other * rows, rows), rows), :],
+            dst_ref=back.at[step, owner],
+            send_sem=back_send.at[step, other],
+            recv_sem=back_recv.at[step, owner],
+            device_id={"band": other},
+            device_id_type=MESH,
+        )
+
+    def along_rows(step):
+        for d in range(1, band_size):
+            other = lax.rem(me + d, band_size)
+            block_copy(step, other, other, other).wait_recv()
+        own_copy(step).wait()
+        s_high, s_low = halves(recv[step])
+        both = jnp.concatenate([s_high, s_low], axis=1)
+
+        def row_tile(j, carry):
+            at = pl.multiple_of(j * tile, tile)
+            one = jnp.dot(high[pl.ds(at, tile), :], both, preferred_element_type=jnp.float32)
+            two = jnp.dot(low[pl.ds(at, tile), :], s_high, preferred_element_type=jnp.float32)
+            mixed[step, pl.ds(at, tile), :] = one[:, :piece_width] + (one[:, piece_width:] + two)
+            return carry
+
+        lax.fori_loop(0, order // tile, row_tile, 0)
+        for d in range(1, band_size):
+            back_copy(step, me, lax.rem(me + d, band_size)).start()
+        back[step, me] = mixed[step, pl.ds(pl.multiple_of(me * rows, rows), rows), :]
+
     def turn(i, carry):
         @pl.when((i < channels) & (window < tm_size - 1))
         def _():
             propagate(i)
             tm_copy(i, window + 1).start()
 
-        @pl.when(i >= LAG)
+        @pl.when((i >= LAG) & (i < channels + LAG))
         def _():
             f = i - LAG
             step, part = f // group, lax.rem(f, group)
@@ -229,93 +350,25 @@
                 def _():
                     own_copy(step).start()
 
+        @pl.when(i == 1)
+        def _():
+            pass_to_windows()
+
+        @pl.when(i == 3)
+        def _():
+            pass_to_sibling()
+
+        @pl.when(i == BACK_LAG)
+        def _():
+            split_matrix()
+
+        @pl.when((i >= BACK_LAG) & (lax.rem(i - BACK_LAG + 1, group) == 0))
+        def _():
+            along_rows((i - BACK_LAG) // group)
+
         return carry
 
-    lax.fori_loop(0, channels + LAG, turn, 0)
-
-    def finish(step, carry):
-        for d in range(1, band_size):
-            other = lax.rem(me + d, band_size)
-            block_copy(step, other, me, other).wait_send()
-            block_copy(step, other, other, other).wait_recv()
-        own_copy(step).wait()
-        return carry
-
-    lax.fori_loop(0, steps, finish, 0)
-
-    @pl.when(window < tm_size - 1)
-    def _():
-        def sent(f, carry):
-            tm_copy(f, window + 1).wait_send()
-            return carry
-
-        lax.fori_loop(0, channels, sent, 0)
-
-    @pl.when(me > 0)
-    def _():
-        for copy in halo_copies(1, me - 1):
-            copy.wait_send()
-
-    @pl.when(me < band_size - 1)
-    def _():
-        for copy in halo_copies(0, me + 1):
-            copy.wait_send()
-
-
-def halves(value):
-    high = value.astype(jnp.bfloat16)
-    return high, (value - high.astype(jnp.float32)).astype(jnp.bfloat16)
-
-
-def correlate_kernel(
-    band_size, group,
-    blocks, corr, sig,
-    out,
-    high, low, mixed, back, send_sem, recv_sem,
-):
-    steps, order, piece_width = blocks.shape
-    channels, rows, width = sig.shape
-    pieces = band_size // group
-    me = lax.axis_index("band")
-    tile = min(order, 512)
-
-    greet(band_size, 1, False)
-
-    def split(j, carry):
-        at = pl.multiple_of(j * 64, 64)
-        high[pl.ds(at, 64), :], low[pl.ds(at, 64), :] = halves(corr[pl.ds(at, 64), :])
-        return carry
-
-    lax.fori_loop(0, order // 64, split, 0)
-
-    def block_copy(step, owner, other):
-        return pltpu.make_async_remote_copy(
-            src_ref=mixed.at[step, pl.ds(pl.multiple_of(other * rows, rows), rows), :],
-            dst_ref=back.at[step, owner],
-            send_sem=send_sem.at[step, other],
-            recv_sem=recv_sem.at[step, owner],
-            device_id={"band": other},
-            device_id_type=MESH,
-        )
-
-    def along_rows(step, carry):
-        s_high, s_low = halves(blocks[step])
-        both = jnp.concatenate([s_high, s_low], axis=1)
-
-        def row_tile(j, carry):
-            at = pl.multiple_of(j * tile, tile)
-            one = jnp.dot(high[pl.ds(at, tile), :], both, preferred_element_type=jnp.float32)
-            two = jnp.dot(low[pl.ds(at, tile), :], s_high, preferred_element_type=jnp.float32)
-            mixed[step, pl.ds(at, tile), :] = one[:, :piece_width] + (one[:, piece_width:] + two)
-            return carry
-
-        lax.fori_loop(0, order // tile, row_tile, 0)
-        for d in range(1, band_size):
-            block_copy(step, me, lax.rem(me + d, band_size)).start()
-        back[step, me] = mixed[step, pl.ds(pl.multiple_of(me * rows, rows), rows), :]
-        return carry
-
-    lax.fori_loop(0, steps, along_rows, 0)
+    lax.fori_loop(0, channels + BACK_LAG, turn, 0)
 
     contract_last = (((1,), (1,)), ((), ()))
 
@@ -326,7 +379,7 @@
 
             @pl.when(owner != me)
             def _(owner=owner):
-                block_copy(step, owner, owner).wait_recv()
+                back_copy(step, owner, owner).wait_recv()
 
         value = jnp.concatenate([back[step, part * pieces + p] for p in range(pieces)], axis=1)
         v_high, v_low = halves(value)
@@ -342,10 +395,44 @@
 
     def sent(step, carry):
         for d in range(1, band_size):
-            block_copy(step, me, lax.rem(me + d, band_size)).wait_send()
+            back_copy(step, me, lax.rem(me + d, band_size)).wait_send()
         return carry
 
     lax.fori_loop(0, steps, sent, 0)
+
+    def spread_sent(step, carry):
+        for d in range(1, band_size):
+            other = lax.rem(me + d, band_size)
+            block_copy(step, other, me, other).wait_send()
+        return carry
+
+    lax.fori_loop(0, steps, spread_sent, 0)
+
+    for h in range(1, pairs):
+        share_copy(h, me, onward(h)).wait_send()
+        for g in range(1, sharers):
+            window_copy(h, g, turn_in, base + lax.rem(turn_in + g, sharers)).wait_send()
+    core_copy(0, me).wait_send()
+    for h in range(1, pairs):
+        core_copy(h, source(h)).wait_send()
+
+    @pl.when(window < tm_size - 1)
+    def _():
+        def sent(f, carry):
+            tm_copy(f, window + 1).wait_send()
+            return carry
+
+        lax.fori_loop(0, channels, sent, 0)
+
+    @pl.when(me > 0)
+    def _():
+        for copy in halo_copies(1, me - 1):
+            copy.wait_send()
+
+    @pl.when(me < band_size - 1)
+    def _():
+        for copy in halo_copies(0, me + 1):
+            copy.wait_send()
 
 
 def local(increments, velocity, diffusivity, scaling, correlation):
@@ -363,20 +450,23 @@
     f32 = jnp.float32
     vmem = pl.BlockSpec(memory_space=pltpu.VMEM)
 
-    share = math.gcd(rows, tm_size)
-    if share == tm_size:
-        part = rows // tm_size
-        mine = lax.dynamic_slice_in_dim(correlation, lax.axis_index("tm") * part, part, 0)
-        corr = lax.all_gather(mine, ("band", "tm"), axis=0, tiled=True)
-    else:
-        corr = lax.all_gather(correlation, "band", axis=0, tiled=True)
-
-    blocks = pl.pallas_call(
-        functools.partial(spread_kernel, band_size, tm_size, group),
-        out_shape=jax.ShapeDtypeStruct((steps, order, piece_width), f32),
-        in_specs=[vmem, vmem, pl.BlockSpec(memory_space=pltpu.SMEM), vmem],
-        out_specs=pl.BlockSpec(memory_space=pl.ANY),
+    sharers = min(tm_size, rows // HALO)
+    while tm_size % sharers or rows % (sharers * HALO):
+        sharers -= 1
+    pairs = band_size // 2
+
+    out = pl.pallas_call(
+        functools.partial(defects_kernel, band_size, tm_size, group, sharers),
+        out_shape=jax.ShapeDtypeStruct((channels, rows, width), f32),
+        in_specs=[vmem, vmem, pl.BlockSpec(memory_space=pltpu.SMEM), vmem, vmem],
+        out_specs=vmem,
         scratch_shapes=[
+            pltpu.VMEM((order, order), f32),
+            pltpu.VMEM((order, order), jnp.bfloat16),
+            pltpu.VMEM((order, order), jnp.bfloat16),
+            pltpu.VMEM((steps, order, piece_width), f32),
+            pltpu.VMEM((steps, band_size, rows, piece_width), f32),
+            pltpu.VMEM((steps, order, piece_width), f32),
             pltpu.VMEM((channels, rows, width), f32),
             pltpu.VMEM((channels, rows, width), f32),
             pltpu.VMEM((steps, band_size, rows, piece_width), f32),
@@ -393,37 +483,23 @@
             dma((steps, band_size)),
             dma((steps, band_size)),
             dma((steps,)),
+            dma((steps, band_size)),
+            dma((steps, band_size)),
+            dma((pairs,)),
+            dma((pairs,)),
+            dma((pairs, sharers)),
+            dma((pairs, sharers)),
+            dma((pairs,)),
+            dma((pairs,)),
         ],
         compiler_params=pltpu.CompilerParams(
             collective_id=0, has_side_effects=True, vmem_limit_bytes=VMEM_LIMIT
         ),
         cost_estimate=pl.CostEstimate(
-            flops=200 * channels * rows * width, bytes_accessed=128 * channels * rows * width, transcendentals=0
-        ),
-        name="spread",
-    )(inc, velocity[0], diff, sig)
-
-    out = pl.pallas_call(
-        functools.partial(correlate_kernel, band_size, group),
-        out_shape=jax.ShapeDtypeStruct((channels, rows, width), f32),
-        in_specs=[vmem, vmem, vmem],
-        out_specs=vmem,
-        scratch_shapes=[
-            pltpu.VMEM((order, order), jnp.bfloat16),
-            pltpu.VMEM((order, order), jnp.bfloat16),
-            pltpu.VMEM((steps, order, piece_width), f32),
-            pltpu.VMEM((steps, band_size, rows, piece_width), f32),
-            dma((steps, band_size)),
-            dma((steps, band_size)),
-        ],
-        compiler_params=pltpu.CompilerParams(
-            collective_id=1, has_side_effects=True, vmem_limit_bytes=VMEM_LIMIT
-        ),
-        cost_estimate=pl.CostEstimate(
             flops=12 * channels * rows * width * order, bytes_accessed=16 * channels * rows * width, transcendentals=0
         ),
-        name="correlate",
-    )(blocks, corr, sig)
+        name="defects",
+    )(inc, velocity[0], diff, sig, correlation)
     return out.reshape(1, FIELDS, LEVELS, rows, width)
 
 

time: 261 us -> 237 us (0.908)
  between operations: 13.4 us -> 0.01 us
  Pallas kernels: 238 us -> 231 us
    pallas_call x2 -> x1, Pallas kernels: 238 us -> 231 us  [local(): pl.pallas_call(functools.partial(defects_kernel, band_size, tm_size, grou...]
    unnamed x6 -> x2, local copies, waits for them, and re-layouts: 7.82 us -> 5.55 us
  transfers between devices with their start and end apart: 1 -> 0, of which waited for: 0 -> 0; matrix products, arithmetic and copies ran while one was open for 0% -> 0% of each run, Pallas kernels for 51% -> 0%
where the time goes in v2:
time: 237 us
  Pallas kernels  231 us (97%)
  local copies, waits for them, and re-layouts  6.15 us (3%)
    pallas_call x1, Pallas kernels, local(): pl.pallas_call(functools.partial(defects_kernel, band_size, tm_size, grou...  231 us
    unnamed x2, local copies, waits for them, and re-layouts  5.55 us

profile of v2, /device:TPU:29, one launch (start us, length us, event | category | flops | bytes accessed | tf_op | source)
XLA Modules:
  0.0 237.3 jit_solution(10796675552357723765)
XLA Ops:
  0.0 0.8 copy.7
  0.8 0.6 reshape.13.diff
  1.4 231.1 %defects.1 = f32[8,128,1024]{2,1,0:T(8,128)} custom-call(f32[8,128,1024]{2,1,0:T(8,128)} %bitcast.5, f32[2,128,1024]{2,1,0:T(8,128)} %bitcast.7, f32[8]{0:T(128)} %reshape.13.diff, f32[8,128,1024]{2,1,0:T(8,128)} %bitcast.6, f32[128,1024]{1,0:T(8,128)} %corr.1), custom_call_target="tpu_custom_call" | custom-call | flops 12884901888 | bytes 16777216 | tf_op jit(solution)/shard_map/defects/pallas_call | solution.py:458
  232.5 4.8 %copy.9 = f32[1,4,2,128,1024]{4,3,2,1,0:T(8,128)} copy(f32[1,4,2,128,1024]{4,3,2,1,0:T(8,128)} %bitcast.4) | data formatting | bytes 8388608

commit v3 on v2

--- a/solution.py
+++ b/solution.py
@@ -52,13 +52,14 @@
 
 def defects_kernel(
     band_size, tm_size, group, sharers,
-    inc, vel, diff, sig, corr,
-    out,
+    inc_in, vel_in, diff, sig_in, corr,
+    result,
+    inc, vel, sig, out, vel_load, corr_load, inc_load, sig_load, out_store,
     full, high, low, mixed, back, recv, ends, arrived, scaled, ping, pong, east_speed, north_speed, halo_x, halo_v,
     halo_send, halo_recv, tm_send, tm_recv, a2a_send, a2a_recv, own_sem, back_send, back_recv,
     share_send, share_recv, window_send, window_recv, core_send, core_recv,
 ):
-    channels, rows, width = inc.shape
+    channels, rows, width = inc_in.shape
     pieces = band_size // group
     piece_width = width // pieces
     steps = channels // group
@@ -73,6 +74,27 @@
     sibling = me + 1 - 2 * core
     turn_in = lax.rem(window, sharers)
     base = window - turn_in
+
+    def inc_copy(f):
+        return pltpu.make_async_copy(inc_in.at[f], inc.at[f], inc_load.at[f])
+
+    def sig_copy(f):
+        return pltpu.make_async_copy(sig_in.at[f], sig.at[f], sig_load.at[f])
+
+    def out_copy(f):
+        return pltpu.make_async_copy(out.at[f], result.at[f], out_store.at[f])
+
+    own_rows = pl.ds(pl.multiple_of(me * rows, rows), rows)
+    vel_copy = pltpu.make_async_copy(vel_in, vel, vel_load.at[0])
+    corr_copy = pltpu.make_async_copy(corr, full.at[own_rows, :], corr_load.at[0])
+
+    vel_copy.start()
+
+    def load(f, carry):
+        inc_copy(f).start()
+        return carry
+
+    lax.fori_loop(0, channels, load, 0)
 
     greet(band_size, tm_size, sharers)
 
@@ -87,7 +109,7 @@
                 device_id={"band": neighbour},
                 device_id_type=MESH,
             )
-            for kind, (array, store) in enumerate(((vel, halo_v), (inc, halo_x)))
+            for kind, (array, store) in enumerate(((vel_in, halo_v), (inc_in, halo_x)))
         ]
 
     @pl.when(me > 0)
@@ -148,6 +170,13 @@
         share_copy(h, me, onward(h)).start()
     core_copy(0, me).start()
 
+    def load_scaling(f, carry):
+        sig_copy(f).start()
+        return carry
+
+    lax.fori_loop(0, channels, load_scaling, 0)
+    corr_copy.start()
+
     def pass_to_windows():
         for h in range(1, pairs):
             share_copy(h, source(h), source(h)).wait_recv()
@@ -162,7 +191,7 @@
             core_copy(h, source(h)).start()
 
     def split_matrix():
-        full[band_rows(me), :] = corr[...]
+        corr_copy.wait()
         for h in range(pairs):
             core_copy(h, source(h) + 1 - 2 * core).wait_recv()
 
@@ -194,7 +223,8 @@
         north_speed[pl.ds(at + 2 * HALO, HALO), :] = 0.5 * vel[1, pl.ds(at, HALO), :]
         return carry
 
-    lax.fori_loop(0, rows // HALO, inner_speeds, 0)
+    vel_copy.wait()
+    lax.fori_loop(0, rows // HALO, inner_speeds, 0, unroll=4)
 
     @pl.when(me > 0)
     def _():
@@ -316,6 +346,10 @@
         back[step, me] = mixed[step, pl.ds(pl.multiple_of(me * rows, rows), rows), :]
 
     def turn(i, carry):
+        @pl.when(i < channels)
+        def _():
+            inc_copy(i).wait()
+
         @pl.when((i < channels) & (window < tm_size - 1))
         def _():
             propagate(i)
@@ -325,6 +359,7 @@
         def _():
             f = i - LAG
             step, part = f // group, lax.rem(f, group)
+            sig_copy(f).wait()
 
             @pl.when(window > 0)
             def _():
@@ -389,6 +424,7 @@
             one = lax.dot_general(both, high[cut, :], contract_last, preferred_element_type=jnp.float32)
             two = lax.dot_general(v_high, low[cut, :], contract_last, preferred_element_type=jnp.float32)
             out[f, :, cut] = sig[f, :, cut] * (one[:rows] + (one[rows:] + two))
+        out_copy(f).start()
         return carry
 
     lax.fori_loop(0, channels, along_columns, 0)
@@ -433,6 +469,12 @@
     def _():
         for copy in halo_copies(0, me + 1):
             copy.wait_send()
+
+    def stored(f, carry):
+        out_copy(f).wait()
+        return carry
+
+    lax.fori_loop(0, channels, stored, 0)
 
 
 def local(increments, velocity, diffusivity, scaling, correlation):
@@ -448,7 +490,7 @@
     order = rows * band_size
     dma = pltpu.SemaphoreType.DMA
     f32 = jnp.float32
-    vmem = pl.BlockSpec(memory_space=pltpu.VMEM)
+    held = pl.BlockSpec(memory_space=pl.ANY)
 
     sharers = min(tm_size, rows // HALO)
     while tm_size % sharers or rows % (sharers * HALO):
@@ -458,9 +500,18 @@
     out = pl.pallas_call(
         functools.partial(defects_kernel, band_size, tm_size, group, sharers),
         out_shape=jax.ShapeDtypeStruct((channels, rows, width), f32),
-        in_specs=[vmem, vmem, pl.BlockSpec(memory_space=pltpu.SMEM), vmem, vmem],
-        out_specs=vmem,
+        in_specs=[held, held, pl.BlockSpec(memory_space=pltpu.SMEM), held, held],
+        out_specs=held,
         scratch_shapes=[
+            pltpu.VMEM((channels, rows, width), f32),
+            pltpu.VMEM((2, rows, width), f32),
+            pltpu.VMEM((channels, rows, width), f32),
+            pltpu.VMEM((channels, rows, width), f32),
+            dma((1,)),
+            dma((1,)),
+            dma((channels,)),
+            dma((channels,)),
+            dma((channels,)),
             pltpu.VMEM((order, order), f32),
             pltpu.VMEM((order, order), jnp.bfloat16),
             pltpu.VMEM((order, order), jnp.bfloat16),

time: 237 us -> 233 us (0.983)
  Pallas kernels: 231 us -> 227 us
    pallas_call x1, Pallas kernels: 231 us -> 227 us  [local(): pl.pallas_call(functools.partial(defects_kernel, band_size, tm_size, grou...]
where the time goes in v3:
time: 233 us
  Pallas kernels  227 us (97%)
  local copies, waits for them, and re-layouts  6.15 us (3%)
    pallas_call x1, Pallas kernels, local(): pl.pallas_call(functools.partial(defects_kernel, band_size, tm_size, grou...  227 us
    unnamed x2, local copies, waits for them, and re-layouts  5.55 us

profile of v3, /device:TPU:29, one launch (start us, length us, event | category | flops | bytes accessed | tf_op | source)
XLA Modules:
  0.0 232.7 jit_solution(12929565704741685297)
XLA Ops:
  0.0 0.8 copy.7
  0.8 0.6 reshape.13.diff
  1.4 226.6 %defects.1 = f32[8,128,1024]{2,1,0:T(8,128)} custom-call(f32[8,128,1024]{2,1,0:T(8,128)} %bitcast.5, f32[2,128,1024]{2,1,0:T(8,128)} %bitcast.7, f32[8]{0:T(128)} %reshape.13.diff, f32[8,128,1024]{2,1,0:T(8,128)} %bitcast.6, f32[128,1024]{1,0:T(8,128)} %corr.1), custom_call_target="tpu_custom_call" | custom-call | flops 12884901888 | bytes 16777216 | tf_op jit(solution)/shard_map/defects/pallas_call | solution.py:500
  228.0 4.8 %copy.9 = f32[1,4,2,128,1024]{4,3,2,1,0:T(8,128)} copy(f32[1,4,2,128,1024]{4,3,2,1,0:T(8,128)} %bitcast.4) | data formatting | bytes 8388608

commit v4 on v3

--- a/solution.py
+++ b/solution.py
@@ -13,7 +13,7 @@
 HALO = 8
 LANES = 128
 LAG = 2
-BACK_LAG = 4
+BACK_LAG = 5
 MESH = pl.DeviceIdType.MESH
 VMEM_LIMIT = 60 * 1024 * 1024
 
@@ -385,11 +385,11 @@
                 def _():
                     own_copy(step).start()
 
-        @pl.when(i == 1)
+        @pl.when(i == LAG)
         def _():
             pass_to_windows()
 
-        @pl.when(i == 3)
+        @pl.when(i == BACK_LAG - 1)
         def _():
             pass_to_sibling()
 

time: 233 us -> 233 us (level)
  no operation moved by 1% of the time
where the time goes in v4:
time: 233 us
  Pallas kernels  227 us (97%)
  local copies, waits for them, and re-layouts  6.15 us (3%)
    pallas_call x1, Pallas kernels, local(): pl.pallas_call(functools.partial(defects_kernel, band_size, tm_size, grou...  227 us
    unnamed x2, local copies, waits for them, and re-layouts  5.55 us

profile of v4, /device:TPU:29, one launch (start us, length us, event | category | flops | bytes accessed | tf_op | source)
XLA Modules:
  0.0 232.7 jit_solution(7266256151054079953)
XLA Ops:
  0.0 0.8 copy.7
  0.8 0.6 reshape.13.diff
  1.4 226.6 %defects.1 = f32[8,128,1024]{2,1,0:T(8,128)} custom-call(f32[8,128,1024]{2,1,0:T(8,128)} %bitcast.5, f32[2,128,1024]{2,1,0:T(8,128)} %bitcast.7, f32[8]{0:T(128)} %reshape.13.diff, f32[8,128,1024]{2,1,0:T(8,128)} %bitcast.6, f32[128,1024]{1,0:T(8,128)} %corr.1), custom_call_target="tpu_custom_call" | custom-call | flops 12884901888 | bytes 16777216 | tf_op jit(solution)/shard_map/defects/pallas_call | solution.py:500
  227.9 4.8 %copy.9 = f32[1,4,2,128,1024]{4,3,2,1,0:T(8,128)} copy(f32[1,4,2,128,1024]{4,3,2,1,0:T(8,128)} %bitcast.4) | data formatting | bytes 8388608

commit v5 on v4

--- a/solution.py
+++ b/solution.py
@@ -67,6 +67,7 @@
     window = lax.axis_index("tm")
 
     order = band_size * rows
+    half_rows = rows // 2
     part = rows // sharers
     tile = min(order, 512)
     pairs = band_size // 2
@@ -288,22 +289,23 @@
 
         tangent_step(stores[(STEPS - 1) % 2], k, 2, rows // HALO, put_end)
 
-    def tm_copy(f, other):
+    def tm_copy(f, half, other):
+        at = pl.ds(half * half_rows, half_rows)
         return pltpu.make_async_remote_copy(
-            src_ref=ends.at[f],
-            dst_ref=arrived.at[f],
-            send_sem=tm_send.at[f],
-            recv_sem=tm_recv.at[f],
+            src_ref=ends.at[f, at, :],
+            dst_ref=arrived.at[f, at, :],
+            send_sem=tm_send.at[f, half],
+            recv_sem=tm_recv.at[f, half],
             device_id={"tm": other},
             device_id_type=MESH,
         )
 
-    def block_copy(step, block, owner, other):
+    def block_copy(step, half, block, owner, other):
         return pltpu.make_async_remote_copy(
-            src_ref=scaled.at[step, block],
-            dst_ref=recv.at[step, pl.ds(pl.multiple_of(owner * rows, rows), rows), :],
-            send_sem=a2a_send.at[step, block],
-            recv_sem=a2a_recv.at[step, owner],
+            src_ref=scaled.at[step, block, pl.ds(half * half_rows, half_rows), :],
+            dst_ref=recv.at[step, pl.ds(pl.multiple_of(owner * rows + half * half_rows, half_rows), half_rows), :],
+            send_sem=a2a_send.at[step, half, block],
+            recv_sem=a2a_recv.at[step, half, owner],
             device_id={"band": other},
             device_id_type=MESH,
         )
@@ -328,7 +330,8 @@
     def along_rows(step):
         for d in range(1, band_size):
             other = lax.rem(me + d, band_size)
-            block_copy(step, other, other, other).wait_recv()
+            for half in range(2):
+                block_copy(step, half, other, other, other).wait_recv()
         own_copy(step).wait()
         s_high, s_low = halves(recv[step])
         both = jnp.concatenate([s_high, s_low], axis=1)
@@ -353,7 +356,8 @@
         @pl.when((i < channels) & (window < tm_size - 1))
         def _():
             propagate(i)
-            tm_copy(i, window + 1).start()
+            for half in range(2):
+                tm_copy(i, half, window + 1).start()
 
         @pl.when((i >= LAG) & (i < channels + LAG))
         def _():
@@ -361,29 +365,34 @@
             step, part = f // group, lax.rem(f, group)
             sig_copy(f).wait()
 
-            @pl.when(window > 0)
+            for half in range(2):
+                at = pl.ds(half * half_rows, half_rows)
+
+                @pl.when(window > 0)
+                def _(half=half, at=at):
+                    tm_copy(f, half, window - 1).wait_recv()
+                    for p in range(pieces):
+                        cut = pl.ds(p * piece_width, piece_width)
+                        scaled[step, part * pieces + p, at, :] = sig[f, at, cut] * (
+                            inc[f, at, cut] - arrived[f, at, cut]
+                        )
+
+                @pl.when(window == 0)
+                def _(at=at):
+                    for p in range(pieces):
+                        cut = pl.ds(p * piece_width, piece_width)
+                        scaled[step, part * pieces + p, at, :] = sig[f, at, cut] * inc[f, at, cut]
+
+                for p in range(pieces):
+                    block = part * pieces + lax.rem(me + p, pieces)
+
+                    @pl.when(block != me)
+                    def _(block=block, half=half):
+                        block_copy(step, half, block, me, block).start()
+
+            @pl.when(me // pieces == part)
             def _():
-                tm_copy(f, window - 1).wait_recv()
-                for p in range(pieces):
-                    cut = pl.ds(p * piece_width, piece_width)
-                    scaled[step, part * pieces + p] = sig[f, :, cut] * (inc[f, :, cut] - arrived[f, :, cut])
-
-            @pl.when(window == 0)
-            def _():
-                for p in range(pieces):
-                    cut = pl.ds(p * piece_width, piece_width)
-                    scaled[step, part * pieces + p] = sig[f, :, cut] * inc[f, :, cut]
-
-            for p in range(pieces):
-                block = part * pieces + lax.rem(me + p, pieces)
-
-                @pl.when(block != me)
-                def _(block=block):
-                    block_copy(step, block, me, block).start()
-
-                @pl.when(block == me)
-                def _():
-                    own_copy(step).start()
+                own_copy(step).start()
 
         @pl.when(i == LAG)
         def _():
@@ -439,7 +448,8 @@
     def spread_sent(step, carry):
         for d in range(1, band_size):
             other = lax.rem(me + d, band_size)
-            block_copy(step, other, me, other).wait_send()
+            for half in range(2):
+                block_copy(step, half, other, me, other).wait_send()
         return carry
 
     lax.fori_loop(0, steps, spread_sent, 0)
@@ -455,7 +465,8 @@
     @pl.when(window < tm_size - 1)
     def _():
         def sent(f, carry):
-            tm_copy(f, window + 1).wait_send()
+            for half in range(2):
+                tm_copy(f, half, window + 1).wait_send()
             return carry
 
         lax.fori_loop(0, channels, sent, 0)
@@ -529,10 +540,10 @@
             pltpu.VMEM((2, 2, HALO, width), f32),
             dma((2, 2)),
             dma((2, 2)),
-            dma((channels,)),
-            dma((channels,)),
-            dma((steps, band_size)),
-            dma((steps, band_size)),
+            dma((channels, 2)),
+            dma((channels, 2)),
+            dma((steps, 2, band_size)),
+            dma((steps, 2, band_size)),
             dma((steps,)),
             dma((steps, band_size)),
             dma((steps, band_size)),

time: 233 us -> 235 us (level)
  no operation moved by 1% of the time
where the time goes in v5:
time: 235 us; the launch traced here: 234 us
  Pallas kernels  228 us (97%)
  local copies, waits for them, and re-layouts  6.15 us (3%)
    pallas_call x1, Pallas kernels, local(): pl.pallas_call(functools.partial(defects_kernel, band_size, tm_size, grou...  228 us
    unnamed x2, local copies, waits for them, and re-layouts  5.55 us

profile of v5, /device:TPU:29, one launch (start us, length us, event | category | flops | bytes accessed | tf_op | source)
XLA Modules:
  0.0 234.3 jit_solution(16362967688799327987)
XLA Ops:
  0.0 0.8 copy.7
  0.8 0.6 reshape.13.diff
  1.4 228.2 %defects.1 = f32[8,128,1024]{2,1,0:T(8,128)} custom-call(f32[8,128,1024]{2,1,0:T(8,128)} %bitcast.5, f32[2,128,1024]{2,1,0:T(8,128)} %bitcast.7, f32[8]{0:T(128)} %reshape.13.diff, f32[8,128,1024]{2,1,0:T(8,128)} %bitcast.6, f32[128,1024]{1,0:T(8,128)} %corr.1), custom_call_target="tpu_custom_call" | custom-call | flops 12884901888 | bytes 16777216 | tf_op jit(solution)/shard_map/defects/pallas_call | solution.py:511
  229.6 4.8 %copy.9 = f32[1,4,2,128,1024]{4,3,2,1,0:T(8,128)} copy(f32[1,4,2,128,1024]{4,3,2,1,0:T(8,128)} %bitcast.4) | data formatting | bytes 8388608
